TPU v7x, 512 devices: a whole 4x8x8 slice. The times are simulated.
512 devices in a mesh: tok: 32 (over y, x), kv: 16 (over z, core).
Axes of the slice: x: 4, y: 8, z: 8, core: 2. Of those that a mesh axis runs over, the one named last changes fastest.
Arguments:
- hidden_in: bfloat16 [32768, 1024], P(('tok', 'kv')), may hold values from -12 to 12
- qkv_weight: bfloat16 [1024, 3, 1024], P(None, None, 'kv'), may hold values from -1 to 1
- stretch_len: int32 [48], replicated, may hold values from 1 to 1024, 32768 in all
- out_weight: bfloat16 [1024, 1024], P('kv'), may hold values from -0.1875 to 0.1875
- ln1_gain: float32 [1024], replicated, may hold values from 0.5 to 1.5
- ln1_bias: float32 [1024], replicated, may hold values from -3 to 3
- up_weight: bfloat16 [1024, 4096], P(None, 'kv'), may hold values from -0.1875 to 0.1875
- down_weight: bfloat16 [4096, 1024], P('kv'), may hold values from -0.09375 to 0.09375
- ln2_gain: float32 [1024], replicated, may hold values from 0.5 to 1.5
- ln2_bias: float32 [1024], replicated, may hold values from -3 to 3
- dec_query: bfloat16 [1024, 1024], P(('tok', 'kv')), may hold values from -12 to 12
- kv_cache: bfloat16 [2, 32, 96, 128, 1024], P(None, 'tok', 'kv'), may hold values from -12 to 12
- piece_req: int32 [32, 96], P('tok', 'kv'), may hold values from 0 to 31, as said below
- piece_used: int32 [32, 96], P('tok', 'kv'), may hold values from 0 to 128, as said below
Outputs:
- prefill_out: bfloat16 [32768, 1024], P(('tok', 'kv'))
- dec_out: bfloat16 [1024, 1024], P(('tok', 'kv'))
Inputs may be any that keep to these rules, and one draw needn't show every extreme that they name: `piece_req`: every request of an index of tok owns at least one piece of that index with a nonzero count. `piece_used`: slots with a count of 0 hold no tokens.
All inputs are finite; a program needn't handle non-finite values.
Results may differ from a plain program's by a relative error of at most 0.017.
Values may be sent and summed in bfloat16 or wider, within the bound.
A program may use at most 64 MiB of HBM per device.

v0:
```python
import math
import jax
import jax.numpy as jnp
from jax import lax
from jax.sharding import PartitionSpec as P

H = 16
HD = 64
WIN = 512
PLEN = 128
NEG_FILL = -1e30
LN_EPS = 1e-05


def extended(value, sides, width):
    for axis, dim in sides:
        count, length = (lax.axis_size(axis), value.shape[dim])
        up = [(i, (i + 1) % count) for i in range(count - 1)]
        down = [(j, i) for i, j in up]
        last = lax.slice_in_dim(value, length - width, length, axis=dim)
        leading = lax.slice_in_dim(value, 0, width, axis=dim)
        before = lax.ppermute(last, axis, up)
        after = lax.ppermute(leading, axis, down)
        value = jnp.concatenate([before, value, after], axis=dim)
    return value


def merged(value, axis, join):
    pieces = jax.tree.map(lambda part: lax.all_gather(part, axis), value)
    head = jax.tree.map(lambda part: part[0], pieces)
    tail = jax.tree.map(lambda part: part[1:], pieces)
    subtotal, _ = lax.scan(lambda subtotal, section: (join(subtotal, section), None), head, tail)
    return subtotal


def segment_ids(row_ids, stretch_len):
    stretch_ends = jnp.cumsum(stretch_len)
    return jnp.sum((row_ids[:, None] >= stretch_ends[None, :]).astype(jnp.int32), axis=1)


def layer_norm(values, gain, bias):
    center = values - jnp.mean(values, axis=1, keepdims=True)
    spread = jnp.mean(center * center, axis=1, keepdims=True)
    return center * lax.rsqrt(spread + LN_EPS) * gain + bias


def merge_partials(earlier, later):
    highest = jnp.maximum(earlier[0], later[0])
    left_factor = jnp.exp(earlier[0] - highest)
    right_factor = jnp.exp(later[0] - highest)
    totals = earlier[1] * left_factor + later[1] * right_factor
    weighted = earlier[2] * left_factor[..., None] + later[2] * right_factor[..., None]
    return (highest, totals, weighted)


def row_folder(source, shard_rows):
    return jnp.dot(source, shard_rows, preferred_element_type=jnp.float32)


def body(
    hidden_in,
    qkv_weight,
    stretch_len,
    out_weight,
    ln1_gain,
    ln1_bias,
    up_weight,
    down_weight,
    ln2_gain,
    ln2_bias,
    dec_query,
    kv_cache,
    piece_req,
    piece_used,
):
    inv_scale = 1.0 / math.sqrt(HD)
    reach = WIN // 2
    local_width = qkv_weight.shape[2]
    head_count = local_width // HD
    flat_weight = qkv_weight.reshape(qkv_weight.shape[0], 3 * local_width)
    qkv_rows = jnp.dot(
        lax.all_gather(hidden_in, "kv", axis=0, tiled=True),
        flat_weight,
        preferred_element_type=jnp.float32,
    ).astype(jnp.bfloat16)
    row_count = qkv_rows.shape[0]
    query_rows = qkv_rows[:, :local_width]
    keyval_rows = qkv_rows[:, local_width:]
    padded = extended(keyval_rows, (("tok", 0),), reach)
    first_row = lax.axis_index("tok") * row_count
    total_rows = row_count * lax.axis_size("tok")
    qblock = min(512, row_count)
    span = qblock + 2 * reach
    block_count = row_count // qblock

    def attend(block_index):
        start = block_index * qblock
        query_ids = first_row + start + jnp.arange(qblock, dtype=jnp.int32)
        key_ids = first_row + start - reach + jnp.arange(span, dtype=jnp.int32)
        query_seg = segment_ids(query_ids, stretch_len)
        inside = (key_ids >= 0) & (key_ids < total_rows)
        key_seg = jnp.where(inside, segment_ids(key_ids, stretch_len), -1)
        allowed = (key_seg[None, :] == query_seg[:, None]) & (
            jnp.abs(key_ids[None, :] - query_ids[:, None]) <= reach
        )
        queries = lax.dynamic_slice_in_dim(query_rows, start, qblock, 0).reshape(
            qblock, head_count, HD
        )
        both = lax.dynamic_slice_in_dim(padded, start, span, 0)
        key_rows = both[:, :local_width].reshape(span, head_count, HD)
        value_rows = both[:, local_width:].reshape(span, head_count, HD)
        scores = (
            jnp.einsum("ihd,jhd->hij", queries, key_rows, preferred_element_type=jnp.float32)
            * inv_scale
        )
        scores = jnp.where(allowed[None], scores, NEG_FILL)
        row_max = jnp.max(scores, axis=2, keepdims=True)
        weights = jnp.where(allowed[None], jnp.exp(scores - row_max), 0.0)
        totals = jnp.sum(weights, axis=2)
        summed = jnp.einsum(
            "hij,jhd->ihd",
            weights.astype(jnp.bfloat16),
            value_rows,
            preferred_element_type=jnp.float32,
        )
        return (
            (summed / jnp.transpose(totals)[:, :, None])
            .astype(jnp.bfloat16)
            .reshape(qblock, local_width)
        )

    attention = lax.map(attend, jnp.arange(block_count, dtype=jnp.int32)).reshape(
        row_count, local_width
    )
    token_major = lax.all_to_all(attention, "kv", split_axis=0, concat_axis=1, tiled=True)
    projected = row_folder(token_major, lax.all_gather(out_weight, "kv", axis=0, tiled=True))
    normed = layer_norm(hidden_in.astype(jnp.float32) + projected, ln1_gain, ln1_bias).astype(
        jnp.bfloat16
    )
    units = jax.nn.gelu(
        jnp.dot(
            lax.all_gather(normed, "kv", axis=0, tiled=True),
            up_weight,
            preferred_element_type=jnp.float32,
        ),
        approximate=False,
    ).astype(jnp.bfloat16)
    ffn = lax.psum_scatter(
        jnp.dot(units, down_weight, preferred_element_type=jnp.float32).astype(jnp.bfloat16),
        "kv",
        scatter_dimension=0,
        tiled=True,
    ).astype(jnp.float32)
    prefill_out = layer_norm(normed.astype(jnp.float32) + ffn, ln2_gain, ln2_bias).astype(
        jnp.bfloat16
    )
    group_queries = lax.all_gather(dec_query, "kv", axis=0, tiled=True)
    request_count = group_queries.shape[0]
    owners = piece_req[0]
    filled = piece_used[0]
    slot_count = owners.shape[0]
    request_ids = jnp.arange(request_count, dtype=jnp.int32)
    selector = (owners[:, None] == request_ids[None, :]).astype(jnp.bfloat16)
    chosen = jnp.dot(selector, group_queries, preferred_element_type=jnp.float32).astype(
        jnp.bfloat16
    )
    chosen = chosen.reshape(slot_count, H, HD)
    cache_keys = kv_cache[0, 0].reshape(slot_count, PLEN, H, HD)
    cache_values = kv_cache[1, 0].reshape(slot_count, PLEN, H, HD)
    piece_scores = (
        jnp.einsum("phd,pthd->pht", chosen, cache_keys, preferred_element_type=jnp.float32)
        * inv_scale
    )
    active = jnp.arange(PLEN, dtype=jnp.int32)[None, :] < filled[:, None]
    piece_scores = jnp.where(active[:, None, :], piece_scores, NEG_FILL)
    piece_max = jnp.max(piece_scores, axis=2)
    piece_weights = jnp.where(
        active[:, None, :], jnp.exp(piece_scores - piece_max[:, :, None]), 0.0
    )
    piece_totals = jnp.sum(piece_weights, axis=2)
    partial_value = jnp.einsum(
        "pht,pthd->phd",
        piece_weights.astype(jnp.bfloat16),
        cache_values,
        preferred_element_type=jnp.float32,
    )
    member = (owners[None, :] == request_ids[:, None]) & (filled[None, :] > 0)
    highest = jnp.max(jnp.where(member[:, :, None], piece_max[None], NEG_FILL), axis=1)
    factor = jnp.where(member[:, :, None], jnp.exp(piece_max[None] - highest[:, None, :]), 0.0)
    denom = jnp.sum(factor * piece_totals[None], axis=1)
    weighted = jnp.einsum("rph,phd->rhd", factor, partial_value)
    own_requests = dec_query.shape[0]
    joined = merged((highest, denom, weighted), "kv", merge_partials)
    begin = lax.axis_index("kv") * own_requests
    final_denom = lax.dynamic_slice_in_dim(joined[1], begin, own_requests, 0)
    final_weighted = lax.dynamic_slice_in_dim(joined[2], begin, own_requests, 0)
    dec_out = (
        (final_weighted / final_denom[:, :, None])
        .astype(jnp.bfloat16)
        .reshape(own_requests, H * HD)
    )
    return (prefill_out, dec_out)


def solution(mesh):
    placed = (
        P(("tok", "kv"), None),
        P(None, None, "kv"),
        P(),
        P("kv", None),
        P(),
        P(),
        P(None, "kv"),
        P("kv", None),
        P(),
        P(),
        P(("tok", "kv"), None),
        P(None, "tok", "kv", None, None),
        P("tok", "kv"),
        P("tok", "kv"),
    )
    return jax.shard_map(
        body,
        mesh=mesh,
        in_specs=placed,
        out_specs=(P(("tok", "kv"), None), P(("tok", "kv"), None)),
        check_vma=False,
    )
```

profile of v0, /device:TPU:2, one launch (start us, length us, event | category | flops | bytes accessed | tf_op | source)
XLA Modules:
  0.0 271.2 jit_solution(17714774776569042649)
XLA Ops:
  8.7 3.5 %fusion.114 = (bf16[1,1,6,128,1024]{4,3,2,1,0:T(8,128)(2,1)S(1)}, bf16[1,1,6,128,1024]{4,3,2,1,0:T(8,128)(2,1)}) fusion(bf16[2,1,6,128,1024]{4,3,2,1,0:T(8,128)(2,1)} %param.29), kind=kLoop, calls=%fused_computation.162 | loop fusion | bytes 6291456 | tf_op jit(solution)/shard_map/slice | solution.py:169
  12.2 2.6 copy.71
  14.8 23.3 %all-gather.3 = bf16[16,2,1024]{2,1,0:T(2,128)(2,1)S(1)} all-gather(bf16[1,2,1024]{2,1,0:T(2,128)(2,1)S(1)} %bitcast.103), channel_id=1, replica_groups=mesh['tok'=32,'kv'=16] {'kv'}, dimensions={0}, use_global_device_ids=true | all-gather | bytes 69632 | tf_op jit(solution)/shard_map/all_gather | solution.py:157
  38.5 1.9 fusion.119
  40.6 1.6 copy.72
  42.6 2.3 fusion.70
  44.9 13.0 %all-gather.11.cloned.1.call-done = bf16[1024,1024]{1,0:T(8,128)(2,1)} async-done(((bf16[64,1024]{1,0:T(8,128)(2,1)}), bf16[1024,1024]{1,0:T(8,128)(2,1)}) %all-gather.11.cloned.1.call-update) | async-done | bytes 2097168 | tf_op jit(solution)/shard_map/all_gather | solution.py:82
  57.9 2.4 convolution_convert_fusion.1
  60.3 3.4 %collective-permute-start = (bf16[256,128]{0,1:T(8,128)(2,1)S(1)}, bf16[256,128]{0,1:T(8,128)(2,1)S(1)}, u32[]{:S(2)}, u32[]{:S(2)}) collective-permute-start(bf16[256,128]{0,1:T(8,128)(2,1)S(1)} %get-tuple-element.226), channel_id=1, source_target_pairs={{0,16},{16,32},{32,48},{48,64},{64,80},{80,96},{96,112},{112,128},... | collective-permute-start | bytes 196616 | tf_op jit(solution)/shard_map/ppermute | solution.py:22
  63.7 2.5 collective-permute-start.1
  67.7 2.2 collective-permute-done.1
  69.9 9.1 %while.26 = (s32[]{:T(128)}, bf16[2,512,64]{1,2,0:T(8,128)(2,1)S(1)}, s32[2]{0:T(128)S(1)}, bf16[1536,128]{0,1:T(8,128)(2,1)S(1)}, s32[]{:T(128)}, /*index=5*/s3...) while((s32[]{:T(128)}, ...), condition=%wide.region_6.7_spmd, body=%wide.region_1.6_spmd.sunk | while | flops 149188608 | bytes 6759068 | solution.py:132
  79.8 13.5 %all_to_all.19 = bf16[16,2,2048]{2,1,0:T(2,128)(2,1)S(1)} all-to-all(bf16[16,2,2048]{2,1,0:T(2,128)(2,1)S(1)} %reshape.209), channel_id=1, replica_groups=mesh['tok'=32,'kv'=16] {'kv'}, dimensions={0} | all-to-all | bytes 262144 | tf_op jit(solution)/shard_map/all_to_all | solution.py:135
  93.5 8.7 %all-gather.13.cloned.1.call-done = bf16[1024,1024]{1,0:T(8,128)(2,1)} async-done(((bf16[64,1024]{1,0:T(8,128)(2,1)}), bf16[1024,1024]{1,0:T(8,128)(2,1)}) %all-gather.13.cloned.1.call-update) | async-done | bytes 2097168 | tf_op jit(solution)/shard_map/all_gather | solution.py:136
  102.2 2.2 fusion.116
  105.7 16.5 %all-gather.5 = f32[16,32,16]{1,2,0:T(8,128)S(1)} all-gather(f32[1,32,16]{1,2,0:T(8,128)S(1)} %bitcast.102), channel_id=3, replica_groups=mesh['tok'=32,'kv'=16] {'kv'}, dimensions={0}, use_global_device_ids=true | all-gather | bytes 34816 | tf_op jit(solution)/shard_map/all_gather | solution.py:29
  122.2 15.1 %all-gather.4 = f32[16,32,16]{1,2,0:T(8,128)S(1)} all-gather(f32[1,32,16]{1,2,0:T(8,128)S(1)} %bitcast.99), channel_id=2, replica_groups=mesh['tok'=32,'kv'=16] {'kv'}, dimensions={0}, use_global_device_ids=true | all-gather | bytes 34816 | tf_op jit(solution)/shard_map/all_gather | solution.py:29
  137.3 10.7 %all-gather.17.cloned.1.call-done = f32[512,16,64]{2,0,1:T(8,128)} async-done(((f32[32,16,64]{2,0,1:T(8,128)}), f32[512,16,64]{2,0,1:T(8,128)}) %all-gather.17.cloned.1.call-update) | async-done | bytes 2097168 | tf_op jit(solution)/shard_map/all_gather | solution.py:29
  149.1 4.3 %slice.81 = f32[480,16,64]{2,0,1:T(8,128)} slice(f32[512,16,64]{2,0,1:T(8,128)} %all-gather.17.cloned.1.call-done), slice={[32:512], [0:16], [0:64]} | slice | bytes 3932160 | tf_op jit(solution)/shard_map/slice | solution.py:31
  153.4 38.8 %all-gather.15.cloned.1.call-done = bf16[1024,1024]{1,0:T(8,128)(2,1)} async-done(((bf16[64,1024]{1,0:T(8,128)(2,1)}), bf16[1024,1024]{1,0:T(8,128)(2,1)}) %all-gather.15.cloned.1.call-update) | async-done | bytes 2097168 | tf_op jit(solution)/shard_map/all_gather | solution.py:142
  192.3 7.2 %convolution_convert_fusion = bf16[1024,1024]{1,0:T(8,128)(2,1)} fusion(bf16[256,1024]{1,0:T(8,128)(2,1)S(1)} %copy-done, bf16[1024,1024]{1,0:T(8,128)(2,1)} %all-gather.15.cloned.1.call-done, bf16[1024,256]{1,0:T(8,128)(2,1)S(1)} %copy-done.10), kind=kOutput, calls=%fused_computation.38 | convolution fusion | flops 1091829760 | bytes 5242880 | tf_op jit(solution)/shard_map/dot_general | solution.py:149
  200.4 22.1 %while.27 = (s32[]{:T(128)}, f32[32,16]{0,1:T(8,128)S(1)}, f32[32,16]{0,1:T(8,128)S(1)}, f32[32,16,64]{2,1,0:T(8,128)S(1)}, f32[15,32,16]{1,2,0:T(8,128)S(1)}, /...) while((s32[]{:T(128)}, f32[32,16]{0,1:T(8,128)S(1)}, f32[32,16]{0,1:T(8,128)S(1)}, ...), condition=%wide.region_17.18_spmd, body=%wide.region_16.17_spmd.sunk | while | flops 101378 | bytes 684125 | solution.py:32
  223.4 37.2 %reduce-scatter.2.cloned.1.call-done = bf16[64,1024]{1,0:T(8,128)(2,1)} async-done(((bf16[1024,1024]{1,0:T(8,128)(2,1)}), bf16[64,1024]{1,0:T(8,128)(2,1)}) %reduce-scatter.2.cloned.1.call-update) | async-done | bytes 131088 | tf_op jit(solution)/shard_map/reduce_scatter | solution.py:148
  263.0 1.7 add_convert_fusion
  (177 shorter events, 40.7 us)
Async XLA Ops:
  7.2 185.1 %copy-start = (bf16[256,1024]{1,0:T(8,128)(2,1)S(1)}, bf16[256,1024]{1,0:T(8,128)(2,1)}, u32[]{:S(2)}) copy-start(bf16[256,1024]{1,0:T(8,128)(2,1)} %param.25) | copy-start | bytes 1572868
  7.2 50.7 %all-gather.11.cloned.1.call-start = ((), (), s32[]{:S(2)}) async-start(), calls=%async_computation.2 | async-start | bytes 2228224 | tf_op jit(solution)/shard_map/all_gather | solution.py:82
  7.9 94.3 %all-gather.13.cloned.1.call-start = ((), (), s32[]{:S(2)}) async-start(), calls=%async_computation.3 | async-start | bytes 2228224 | tf_op jit(solution)/shard_map/all_gather | solution.py:136
  8.7 139.3 %all-gather.17.cloned.1.call-start = ((), (), s32[]{:S(2)}) async-start(), calls=%async_computation.6 | async-start | bytes 4456448 | tf_op jit(solution)/shard_map/all_gather | solution.py:29
  12.2 2.6 copy-start.8
  12.2 26.0 %copy-start.9 = (s32[1,6]{1,0:T(1,128)S(1)}, s32[1,6]{1,0:T(1,128)}, u32[]{:S(2)}) copy-start(s32[1,6]{1,0:T(1,128)} %param.30) | copy-start | bytes 76
  12.2 26.3 %copy-start.12 = (s32[1,6]{1,0:T(1,128)S(1)}, s32[1,6]{1,0:T(1,128)}, u32[]{:S(2)}) copy-start(s32[1,6]{1,0:T(1,128)} %param.31) | copy-start | bytes 76
  40.6 17.2 %copy-start.11 = (bf16[1024,3,64]{0,2,1:T(8,128)(2,1)S(1)}, bf16[1024,3,64]{0,2,1:T(8,128)(2,1)}, u32[]{:S(2)}) copy-start(bf16[1024,3,64]{0,2,1:T(8,128)(2,1)} %param.19) | copy-start | bytes 1179652
  57.9 9.5 %copy-start.13 = (s32[48]{0:T(128)S(1)}, s32[48]{0:T(128)}, u32[]{:S(2)}) copy-start(s32[48]{0:T(128)} %param.20) | copy-start | bytes 580
  60.3 7.3 %collective-permute-start = (bf16[256,128]{0,1:T(8,128)(2,1)S(1)}, bf16[256,128]{0,1:T(8,128)(2,1)S(1)}, u32[]{:S(2)}, u32[]{:S(2)}) collective-permute-start(bf16[256,128]{0,1:T(8,128)(2,1)S(1)} %get-tuple-element.226), channel_id=1, source_target_pairs={{0,16},{16,32},{32,48},{48,64},{64,80},{80,96},{96,112},{112,128},... | collective-permute-start | bytes 196616 | tf_op jit(solution)/shard_map/ppermute | solution.py:22
  63.7 6.2 %collective-permute-start.1 = (bf16[256,128]{0,1:T(8,128)(2,1)S(1)}, bf16[256,128]{0,1:T(8,128)(2,1)S(1)}, u32[]{:S(2)}, u32[]{:S(2)}) collective-permute-start(bf16[256,128]{0,1:T(8,128)(2,1)S(1)} %get-tuple-element.227), channel_id=1, source_target_pairs={{16,0},{32,16},{48,32},{64,48},{80,64},{96,80},{112,96},{128,112},... | collective-permute-start | bytes 196616 | tf_op jit(solution)/shard_map/ppermute | solution.py:23
  67.3 124.9 %all-gather.15.cloned.1.call-start = ((), (), s32[]{:S(2)}) async-start(), calls=%async_computation.4 | async-start | bytes 2228224 | tf_op jit(solution)/shard_map/all_gather | solution.py:142
  79.0 23.2 %copy-start.1 = (bf16[64,1024]{1,0:T(8,128)(2,1)S(1)}, bf16[64,1024]{1,0:T(8,128)(2,1)}, u32[]{:S(2)}) copy-start(bf16[64,1024]{1,0:T(8,128)(2,1)} %param.18) | copy-start | bytes 393220
  79.5 25.1 %copy-start.4 = (f32[1024]{0:T(1024)S(1)}, f32[1024]{0:T(1024)}, u32[]{:S(2)}) copy-start(f32[1024]{0:T(1024)} %param.23) | copy-start | bytes 12292
  79.5 25.1 %copy-start.5 = (f32[1024]{0:T(1024)S(1)}, f32[1024]{0:T(1024)}, u32[]{:S(2)}) copy-start(f32[1024]{0:T(1024)} %param.22) | copy-start | bytes 12292
  105.5 155.2 %reduce-scatter.2.cloned.1.call-start = ((), (), s32[]{:S(2)}) async-start(), calls=%async_computation.5 | async-start | bytes 2228224 | tf_op jit(solution)/shard_map/reduce_scatter | solution.py:148
  122.2 31.2 %copy-start.2 = (f32[16,32,16]{1,2,0:T(8,128)}, f32[16,32,16]{1,2,0:T(8,128)S(1)}, u32[]{:S(2)}) copy-start(f32[16,32,16]{1,2,0:T(8,128)S(1)} %all-gather.5) | copy-start | bytes 98308
  137.3 16.1 %copy-start.3 = (f32[16,32,16]{1,2,0:T(8,128)}, f32[16,32,16]{1,2,0:T(8,128)S(1)}, u32[]{:S(2)}) copy-start(f32[16,32,16]{1,2,0:T(8,128)S(1)} %all-gather.4) | copy-start | bytes 98308
  149.1 43.2 %copy-start.10 = (bf16[1024,256]{1,0:T(8,128)(2,1)S(1)}, bf16[1024,256]{1,0:T(8,128)(2,1)}, u32[]{:S(2)}) copy-start(bf16[1024,256]{1,0:T(8,128)(2,1)} %param.24) | copy-start | bytes 1572868
  199.4 0.9 slice-start
  199.4 1.0 slice-start.1
  200.4 62.6 %copy-start.6 = (f32[1024]{0:T(1024)S(1)}, f32[1024]{0:T(1024)}, u32[]{:S(2)}) copy-start(f32[1024]{0:T(1024)} %param.27) | copy-start | bytes 12292
  200.4 62.6 %copy-start.7 = (f32[1024]{0:T(1024)S(1)}, f32[1024]{0:T(1024)}, u32[]{:S(2)}) copy-start(f32[1024]{0:T(1024)} %param.26) | copy-start | bytes 12292
Sparse Core Ops, SparseCore 0:
  10.1 47.6 all-gather.10
  60.0 42.1 all-gather.12
  104.4 43.5 all-gather.16
  150.5 41.7 all-gather.14
  199.6 60.9 reduce-scatter.1
where the time goes:
time: 272 us; the launch traced here: 271 us
  waiting for transfers between devices  112 us (41%)
  blocking collectives  68.4 us (25%)
  local copies, waits for them, and re-layouts  34.2 us (13%)
  matrix products  21.3 us (8%)
  between operations  14.1 us (5%)
  other arithmetic  13.3 us (5%)
  starting transfers between devices  6.04 us (2%)
    all_gather x1, waiting for transfers between devices, body(): lax.all_gather(normed, 'kv', axis=0, tiled=True)  38.8 us
    reduce_scatter x1, waiting for transfers between devices, body(): lax.psum_scatter(jnp.dot(units, down_weight, preferred_element_type=jnp.f...  37.2 us
    all_gather x2, blocking collectives, merged(): pieces = jax.tree.map(lambda part: lax.all_gather(part, axis), value)  31.6 us
    all_gather x1, blocking collectives, body(): group_queries = lax.all_gather(dec_query, 'kv', axis=0, tiled=True)  23.3 us
    dynamic_slice x15, local copies, waits for them, and re-layouts, merged(): lax.scan(lambda subtotal, section: (join(subtotal, section), None), head,...  14.6 us
    all_to_all x1, blocking collectives, body(): lax.all_to_all(attention, 'kv', split_axis=0, concat_axis=1, tiled=True)  13.5 us
    all_gather x1, waiting for transfers between devices, body(): lax.all_gather(hidden_in, 'kv', axis=0, tiled=True)  13 us
    all_gather x1, waiting for transfers between devices, merged(): pieces = jax.tree.map(lambda part: lax.all_gather(part, axis), value)  10.7 us
  transfers between devices with their start and end apart: 7, of which 6 were waited for; matrix products, arithmetic and copies ran while one was open for 21% of the time, Pallas kernels for 0%

commit v1 on v0

--- a/solution.py
+++ b/solution.py
@@ -10,6 +10,19 @@
 PLEN = 128
 NEG_FILL = -1e30
 LN_EPS = 1e-05
+
+
+def gather_around(x, axis, dim):
+    ways = lax.axis_size(axis)
+    up = [(d, (d + 1) % ways) for d in range(ways)]
+    down = [(d, (d - 1) % ways) for d in range(ways)]
+    earlier, later = ([x], [x])
+    for _ in range(ways // 2):
+        earlier.append(lax.ppermute(earlier[-1], axis, up))
+    for _ in range((ways - 1) // 2):
+        later.append(lax.ppermute(later[-1], axis, down))
+    line = jnp.concatenate([*earlier[::-1], *later[1:]], axis=dim)
+    return jnp.roll(line, (lax.axis_index(axis) - ways // 2) * x.shape[dim], axis=dim)
 
 
 def extended(value, sides, width):
@@ -79,9 +92,7 @@
     head_count = local_width // HD
     flat_weight = qkv_weight.reshape(qkv_weight.shape[0], 3 * local_width)
     qkv_rows = jnp.dot(
-        lax.all_gather(hidden_in, "kv", axis=0, tiled=True),
-        flat_weight,
-        preferred_element_type=jnp.float32,
+        gather_around(hidden_in, "kv", 0), flat_weight, preferred_element_type=jnp.float32
     ).astype(jnp.bfloat16)
     row_count = qkv_rows.shape[0]
     query_rows = qkv_rows[:, :local_width]

time: 272 us -> 260 us (0.956)
  waiting for transfers between devices: 112 us -> 81.8 us
  starting transfers between devices: 6.04 us -> 33 us
  blocking collectives: 68.4 us -> 61.5 us
    ppermute x0 -> x15, starting transfers between devices: none -> 27 us  [the longest x7 26.6 us: gather_around(): later.append(lax.ppermute(later[-1], axis, down))]
    ppermute x0 -> x15, waiting for transfers between devices: none -> 17.4 us  [the longest x8 10.1 us: gather_around(): earlier.append(lax.ppermute(earlier[-1], axis, up))]
    all_gather x1, waiting for transfers between devices: 38.8 us -> 24.2 us  [body(): lax.all_gather(normed, 'kv', axis=0, tiled=True)]
    all_gather x1 -> x0, waiting for transfers between devices: 13 us -> none  [body(): lax.all_gather(hidden_in, 'kv', axis=0, tiled=True)]
    all_gather x1, waiting for transfers between devices: 10.7 us -> 0.01 us  [merged(): pieces = jax.tree.map(lambda part: lax.all_gather(part, axis), value)]
    all_gather x1, waiting for transfers between devices: 8.73 us -> 0.02 us  [body(): lax.all_gather(out_weight, 'kv', axis=0, tiled=True)]
    all_gather x1, blocking collectives: 23.3 us -> 16.5 us  [body(): group_queries = lax.all_gather(dec_query, 'kv', axis=0, tiled=True)]
  transfers between devices with their start and end apart: 7 -> 21, of which waited for: 6 -> 14; matrix products, arithmetic and copies ran while one was open for 21% -> 21% of each run, Pallas kernels for 0% -> 0%
where the time goes in v1:
time: 260 us; the launch traced here: 259 us
  waiting for transfers between devices  81.8 us (31%)
  blocking collectives  61.5 us (24%)
  local copies, waits for them, and re-layouts  33.7 us (13%)
  starting transfers between devices  33 us (13%)
  matrix products  19.8 us (8%)
  between operations  14.4 us (6%)
  other arithmetic  13.3 us (5%)
    reduce_scatter x1, waiting for transfers between devices, body(): lax.psum_scatter(jnp.dot(units, down_weight, preferred_element_type=jnp.f...  37.9 us
    all_gather x2, blocking collectives, merged(): pieces = jax.tree.map(lambda part: lax.all_gather(part, axis), value)  31.2 us
    ppermute x7, starting transfers between devices, gather_around(): later.append(lax.ppermute(later[-1], axis, down))  26.6 us
    all_gather x1, waiting for transfers between devices, body(): lax.all_gather(normed, 'kv', axis=0, tiled=True)  24.2 us
    all_gather x1, blocking collectives, body(): group_queries = lax.all_gather(dec_query, 'kv', axis=0, tiled=True)  16.5 us
    dynamic_slice x15, local copies, waits for them, and re-layouts, merged(): lax.scan(lambda subtotal, section: (join(subtotal, section), None), head,...  14.6 us
    all_to_all x1, blocking collectives, body(): lax.all_to_all(attention, 'kv', split_axis=0, concat_axis=1, tiled=True)  13.8 us
    ppermute x8, waiting for transfers between devices, gather_around(): earlier.append(lax.ppermute(earlier[-1], axis, up))  10.1 us
  transfers between devices with their start and end apart: 21, of which 14 were waited for; matrix products, arithmetic and copies ran while one was open for 21% of the time, Pallas kernels for 0%

profile of v1, /device:TPU:2, one launch (start us, length us, event | category | flops | bytes accessed | tf_op | source)
XLA Modules:
  0.0 259.4 jit_solution(4228327412926848676)
XLA Ops:
  7.3 8.5 %collective-permute-start.8 = (bf16[64,1024]{1,0:T(8,128)(2,1)}, bf16[64,1024]{1,0:T(8,128)(2,1)S(1)}, u32[]{:S(2)}, u32[]{:S(2)}) collective-permute-start(bf16[64,1024]{1,0:T(8,128)(2,1)} %param.18), channel_id=1, source_target_pairs={{0,15},{1,0},{2,1},{3,2},{4,3},{5,4},{6,5},{7,6},{8,7},{9,8},{10,9... | collective-permute-start | bytes 393224 | tf_op jit(solution)/shard_map/ppermute | solution.py:23
  15.8 3.5 %fusion.120 = (bf16[1,1,6,128,1024]{4,3,2,1,0:T(8,128)(2,1)S(1)}, bf16[1,1,6,128,1024]{4,3,2,1,0:T(8,128)(2,1)}) fusion(bf16[2,1,6,128,1024]{4,3,2,1,0:T(8,128)(2,1)} %param.29), kind=kLoop, calls=%fused_computation.197 | loop fusion | bytes 6291456 | tf_op jit(solution)/shard_map/slice | solution.py:180
  19.3 2.6 copy.71
  21.9 16.5 %all-gather.3 = bf16[16,2,1024]{2,1,0:T(2,128)(2,1)S(1)} all-gather(bf16[1,2,1024]{2,1,0:T(2,128)(2,1)S(1)} %bitcast.102), channel_id=1, replica_groups=mesh['tok'=32,'kv'=16] {'kv'}, dimensions={0}, use_global_device_ids=true | all-gather | bytes 69632 | tf_op jit(solution)/shard_map/all_gather | solution.py:168
  39.2 5.5 %collective-permute-done.1 = bf16[64,1024]{1,0:T(8,128)(2,1)S(1)} collective-permute-done((bf16[64,1024]{1,0:T(8,128)(2,1)S(1)}, bf16[64,1024]{1,0:T(8,128)(2,1)S(1)}, u32[]{:S(2)}, u32[]{:S(2)}) %collective-permute-start.1) | collective-permute-done | bytes 131104 | tf_op jit(solution)/shard_map/ppermute | solution.py:21
  46.6 3.0 %collective-permute-start.9 = (bf16[64,1024]{1,0:T(8,128)(2,1)S(1)}, bf16[64,1024]{1,0:T(8,128)(2,1)S(1)}, u32[]{:S(2)}, u32[]{:S(2)}) collective-permute-start(bf16[64,1024]{1,0:T(8,128)(2,1)S(1)} %collective-permute-done.8), channel_id=1, source_target_pairs={{0,15},{1,0},{2,1},{3,2},{4,3},{5,4},{6,5},{7,6},{8,7},{9,8},{10,9... | collective-permute-start | bytes 393224 | tf_op jit(solution)/shard_map/ppermute | solution.py:23
  52.9 3.0 %collective-permute-start.10 = (bf16[64,1024]{1,0:T(8,128)(2,1)S(1)}, bf16[64,1024]{1,0:T(8,128)(2,1)S(1)}, u32[]{:S(2)}, u32[]{:S(2)}) collective-permute-start(bf16[64,1024]{1,0:T(8,128)(2,1)S(1)} %collective-permute-done.9), channel_id=1, source_target_pairs={{0,15},{1,0},{2,1},{3,2},{4,3},{5,4},{6,5},{7,6},{8,7},{9,8},{10,9... | collective-permute-start | bytes 393224 | tf_op jit(solution)/shard_map/ppermute | solution.py:23
  58.4 3.1 %collective-permute-start.11 = (bf16[64,1024]{1,0:T(8,128)(2,1)S(1)}, bf16[64,1024]{1,0:T(8,128)(2,1)S(1)}, u32[]{:S(2)}, u32[]{:S(2)}) collective-permute-start(bf16[64,1024]{1,0:T(8,128)(2,1)S(1)} %collective-permute-done.10), channel_id=1, source_target_pairs={{0,15},{1,0},{2,1},{3,2},{4,3},{5,4},{6,5},{7,6},{8,7},{9,8},{10,9... | collective-permute-start | bytes 393224 | tf_op jit(solution)/shard_map/ppermute | solution.py:23
  62.5 2.3 fusion.75
  64.9 3.0 %collective-permute-start.12 = (bf16[64,1024]{1,0:T(8,128)(2,1)S(1)}, bf16[64,1024]{1,0:T(8,128)(2,1)S(1)}, u32[]{:S(2)}, u32[]{:S(2)}) collective-permute-start(bf16[64,1024]{1,0:T(8,128)(2,1)S(1)} %collective-permute-done.11), channel_id=1, source_target_pairs={{0,15},{1,0},{2,1},{3,2},{4,3},{5,4},{6,5},{7,6},{8,7},{9,8},{10,9... | collective-permute-start | bytes 393224 | tf_op jit(solution)/shard_map/ppermute | solution.py:23
  70.4 3.1 %collective-permute-start.13 = (bf16[64,1024]{1,0:T(8,128)(2,1)S(1)}, bf16[64,1024]{1,0:T(8,128)(2,1)S(1)}, u32[]{:S(2)}, u32[]{:S(2)}) collective-permute-start(bf16[64,1024]{1,0:T(8,128)(2,1)S(1)} %collective-permute-done.12), channel_id=1, source_target_pairs={{0,15},{1,0},{2,1},{3,2},{4,3},{5,4},{6,5},{7,6},{8,7},{9,8},{10,9... | collective-permute-start | bytes 393224 | tf_op jit(solution)/shard_map/ppermute | solution.py:23
  76.0 3.1 %collective-permute-start.14 = (bf16[64,1024]{1,0:T(8,128)(2,1)S(1)}, bf16[64,1024]{1,0:T(8,128)(2,1)S(1)}, u32[]{:S(2)}, u32[]{:S(2)}) collective-permute-start(bf16[64,1024]{1,0:T(8,128)(2,1)S(1)} %collective-permute-done.13), channel_id=1, source_target_pairs={{0,15},{1,0},{2,1},{3,2},{4,3},{5,4},{6,5},{7,6},{8,7},{9,8},{10,9... | collective-permute-start | bytes 393224 | tf_op jit(solution)/shard_map/ppermute | solution.py:23
  82.8 3.3 %collective-permute-start.15 = (bf16[256,128]{0,1:T(8,128)(2,1)S(1)}, bf16[256,128]{0,1:T(8,128)(2,1)S(1)}, u32[]{:S(2)}, u32[]{:S(2)}) collective-permute-start(bf16[256,128]{0,1:T(8,128)(2,1)S(1)} %get-tuple-element.226), channel_id=1, source_target_pairs={{0,16},{16,32},{32,48},{48,64},{64,80},{80,96},{96,112},{112,128},... | collective-permute-start | bytes 196616 | tf_op jit(solution)/shard_map/ppermute | solution.py:35
  86.1 2.5 collective-permute-start.16
  92.3 9.1 %while.26 = (s32[]{:T(128)}, bf16[2,512,64]{1,2,0:T(8,128)(2,1)S(1)}, s32[2]{0:T(128)S(1)}, bf16[1536,128]{0,1:T(8,128)(2,1)S(1)}, s32[]{:T(128)}, /*index=5*/s3...) while((s32[]{:T(128)}, ...), condition=%wide.region_6.7_spmd, body=%wide.region_1.6_spmd.sunk | while | flops 149188608 | bytes 6759068 | solution.py:143
  102.1 13.8 %all_to_all.19 = bf16[16,2,2048]{2,1,0:T(2,128)(2,1)S(1)} all-to-all(bf16[16,2,2048]{2,1,0:T(2,128)(2,1)S(1)} %reshape.209), channel_id=1, replica_groups=mesh['tok'=32,'kv'=16] {'kv'}, dimensions={0} | all-to-all | bytes 262144 | tf_op jit(solution)/shard_map/all_to_all | solution.py:146
  116.1 2.2 fusion.122
  119.6 15.2 %all-gather.5 = f32[16,32,16]{1,2,0:T(8,128)S(1)} all-gather(f32[1,32,16]{1,2,0:T(8,128)S(1)} %bitcast.101), channel_id=3, replica_groups=mesh['tok'=32,'kv'=16] {'kv'}, dimensions={0}, use_global_device_ids=true | all-gather | bytes 34816 | tf_op jit(solution)/shard_map/all_gather | solution.py:42
  134.9 16.0 %all-gather.4 = f32[16,32,16]{1,2,0:T(8,128)S(1)} all-gather(f32[1,32,16]{1,2,0:T(8,128)S(1)} %bitcast.98), channel_id=2, replica_groups=mesh['tok'=32,'kv'=16] {'kv'}, dimensions={0}, use_global_device_ids=true | all-gather | bytes 34816 | tf_op jit(solution)/shard_map/all_gather | solution.py:42
  152.0 4.3 %slice.81 = f32[480,16,64]{2,0,1:T(8,128)} slice(f32[512,16,64]{2,0,1:T(8,128)} %all-gather.14.cloned.1.call-done), slice={[32:512], [0:16], [0:64]} | slice | bytes 3932160 | tf_op jit(solution)/shard_map/slice | solution.py:44
  156.3 24.2 %all-gather.12.cloned.1.call-done = bf16[1024,1024]{1,0:T(8,128)(2,1)} async-done(((bf16[64,1024]{1,0:T(8,128)(2,1)}), bf16[1024,1024]{1,0:T(8,128)(2,1)}) %all-gather.12.cloned.1.call-update) | async-done | bytes 2097168 | tf_op jit(solution)/shard_map/all_gather | solution.py:153
  180.6 7.2 %convolution_convert_fusion = bf16[1024,1024]{1,0:T(8,128)(2,1)} fusion(bf16[256,1024]{1,0:T(8,128)(2,1)S(1)} %copy-done, bf16[1024,1024]{1,0:T(8,128)(2,1)} %all-gather.12.cloned.1.call-done, bf16[1024,256]{1,0:T(8,128)(2,1)S(1)} %copy-done.10), kind=kOutput, calls=%fused_computation.40 | convolution fusion | flops 1091829760 | bytes 5242880 | tf_op jit(solution)/shard_map/dot_general | solution.py:160
  187.8 22.1 %while.27 = (s32[]{:T(128)}, f32[32,16]{0,1:T(8,128)S(1)}, f32[32,16]{0,1:T(8,128)S(1)}, f32[32,16,64]{2,1,0:T(8,128)S(1)}, f32[15,32,16]{1,2,0:T(8,128)S(1)}, /...) while((s32[]{:T(128)}, f32[32,16]{0,1:T(8,128)S(1)}, f32[32,16]{0,1:T(8,128)S(1)}, ...), condition=%wide.region_17.18_spmd, body=%wide.region_16.17_spmd.sunk | while | flops 101378 | bytes 684125 | solution.py:45
  210.9 37.9 %reduce-scatter.2.cloned.1.call-done = bf16[64,1024]{1,0:T(8,128)(2,1)} async-done(((bf16[1024,1024]{1,0:T(8,128)(2,1)}), bf16[64,1024]{1,0:T(8,128)(2,1)}) %reduce-scatter.2.cloned.1.call-update) | async-done | bytes 131088 | tf_op jit(solution)/shard_map/reduce_scatter | solution.py:159
  (236 shorter events, 59.4 us)
Async XLA Ops:
  7.2 173.4 %copy-start = (bf16[256,1024]{1,0:T(8,128)(2,1)S(1)}, bf16[256,1024]{1,0:T(8,128)(2,1)}, u32[]{:S(2)}) copy-start(bf16[256,1024]{1,0:T(8,128)(2,1)} %param.25) | copy-start | bytes 1572868
  7.2 108.9 %all-gather.10.cloned.1.call-start = ((), (), s32[]{:S(2)}) async-start(), calls=%async_computation.2 | async-start | bytes 2228224 | tf_op jit(solution)/shard_map/all_gather | solution.py:147
  7.2 31.3 %collective-permute-start = (bf16[64,1024]{1,0:T(8,128)(2,1)}, bf16[64,1024]{1,0:T(8,128)(2,1)S(1)}, u32[]{:S(2)}, u32[]{:S(2)}) collective-permute-start(bf16[64,1024]{1,0:T(8,128)(2,1)} %param.18), channel_id=1, source_target_pairs={{0,1},{1,2},{2,3},{3,4},{4,5},{5,6},{6,7},{7,8},{8,9},{9,10},{10,1... | collective-permute-start | bytes 393224 | tf_op jit(solution)/shard_map/ppermute | solution.py:21
  7.3 39.4 %collective-permute-start.8 = (bf16[64,1024]{1,0:T(8,128)(2,1)}, bf16[64,1024]{1,0:T(8,128)(2,1)S(1)}, u32[]{:S(2)}, u32[]{:S(2)}) collective-permute-start(bf16[64,1024]{1,0:T(8,128)(2,1)} %param.18), channel_id=1, source_target_pairs={{0,15},{1,0},{2,1},{3,2},{4,3},{5,4},{6,5},{7,6},{8,7},{9,8},{10,9... | collective-permute-start | bytes 393224 | tf_op jit(solution)/shard_map/ppermute | solution.py:23
  15.8 135.0 %all-gather.14.cloned.1.call-start = ((), (), s32[]{:S(2)}) async-start(), calls=%async_computation.5 | async-start | bytes 4456448 | tf_op jit(solution)/shard_map/all_gather | solution.py:42
  38.5 6.1 %collective-permute-start.1 = (bf16[64,1024]{1,0:T(8,128)(2,1)S(1)}, bf16[64,1024]{1,0:T(8,128)(2,1)S(1)}, u32[]{:S(2)}, u32[]{:S(2)}) collective-permute-start(bf16[64,1024]{1,0:T(8,128)(2,1)S(1)} %collective-permute-done), channel_id=1, source_target_pairs={{0,1},{1,2},{2,3},{3,4},{4,5},{5,6},{6,7},{7,8},{8,9},{9,10},{10,1... | collective-permute-start | bytes 393224 | tf_op jit(solution)/shard_map/ppermute | solution.py:21
  44.7 6.5 %collective-permute-start.2 = (bf16[64,1024]{1,0:T(8,128)(2,1)S(1)}, bf16[64,1024]{1,0:T(8,128)(2,1)S(1)}, u32[]{:S(2)}, u32[]{:S(2)}) collective-permute-start(bf16[64,1024]{1,0:T(8,128)(2,1)S(1)} %collective-permute-done.1), channel_id=1, source_target_pairs={{0,1},{1,2},{2,3},{3,4},{4,5},{5,6},{6,7},{7,8},{8,9},{9,10},{10,1... | collective-permute-start | bytes 393224 | tf_op jit(solution)/shard_map/ppermute | solution.py:21
  46.6 6.3 %collective-permute-start.9 = (bf16[64,1024]{1,0:T(8,128)(2,1)S(1)}, bf16[64,1024]{1,0:T(8,128)(2,1)S(1)}, u32[]{:S(2)}, u32[]{:S(2)}) collective-permute-start(bf16[64,1024]{1,0:T(8,128)(2,1)S(1)} %collective-permute-done.8), channel_id=1, source_target_pairs={{0,15},{1,0},{2,1},{3,2},{4,3},{5,4},{6,5},{7,6},{8,7},{9,8},{10,9... | collective-permute-start | bytes 393224 | tf_op jit(solution)/shard_map/ppermute | solution.py:23
  51.1 5.8 %collective-permute-start.3 = (bf16[64,1024]{1,0:T(8,128)(2,1)S(1)}, bf16[64,1024]{1,0:T(8,128)(2,1)S(1)}, u32[]{:S(2)}, u32[]{:S(2)}) collective-permute-start(bf16[64,1024]{1,0:T(8,128)(2,1)S(1)} %collective-permute-done.2), channel_id=1, source_target_pairs={{0,1},{1,2},{2,3},{3,4},{4,5},{5,6},{6,7},{7,8},{8,9},{9,10},{10,1... | collective-permute-start | bytes 393224 | tf_op jit(solution)/shard_map/ppermute | solution.py:21
  52.9 5.5 %collective-permute-start.10 = (bf16[64,1024]{1,0:T(8,128)(2,1)S(1)}, bf16[64,1024]{1,0:T(8,128)(2,1)S(1)}, u32[]{:S(2)}, u32[]{:S(2)}) collective-permute-start(bf16[64,1024]{1,0:T(8,128)(2,1)S(1)} %collective-permute-done.9), channel_id=1, source_target_pairs={{0,15},{1,0},{2,1},{3,2},{4,3},{5,4},{6,5},{7,6},{8,7},{9,8},{10,9... | collective-permute-start | bytes 393224 | tf_op jit(solution)/shard_map/ppermute | solution.py:23
  56.9 5.6 %collective-permute-start.4 = (bf16[64,1024]{1,0:T(8,128)(2,1)S(1)}, bf16[64,1024]{1,0:T(8,128)(2,1)S(1)}, u32[]{:S(2)}, u32[]{:S(2)}) collective-permute-start(bf16[64,1024]{1,0:T(8,128)(2,1)S(1)} %collective-permute-done.3), channel_id=1, source_target_pairs={{0,1},{1,2},{2,3},{3,4},{4,5},{5,6},{6,7},{7,8},{8,9},{9,10},{10,1... | collective-permute-start | bytes 393224 | tf_op jit(solution)/shard_map/ppermute | solution.py:21
  58.4 6.5 %collective-permute-start.11 = (bf16[64,1024]{1,0:T(8,128)(2,1)S(1)}, bf16[64,1024]{1,0:T(8,128)(2,1)S(1)}, u32[]{:S(2)}, u32[]{:S(2)}) collective-permute-start(bf16[64,1024]{1,0:T(8,128)(2,1)S(1)} %collective-permute-done.10), channel_id=1, source_target_pairs={{0,15},{1,0},{2,1},{3,2},{4,3},{5,4},{6,5},{7,6},{8,7},{9,8},{10,9... | collective-permute-start | bytes 393224 | tf_op jit(solution)/shard_map/ppermute | solution.py:23
  62.5 5.6 %collective-permute-start.5 = (bf16[64,1024]{1,0:T(8,128)(2,1)S(1)}, bf16[64,1024]{1,0:T(8,128)(2,1)S(1)}, u32[]{:S(2)}, u32[]{:S(2)}) collective-permute-start(bf16[64,1024]{1,0:T(8,128)(2,1)S(1)} %collective-permute-done.4), channel_id=1, source_target_pairs={{0,1},{1,2},{2,3},{3,4},{4,5},{5,6},{6,7},{7,8},{8,9},{9,10},{10,1... | collective-permute-start | bytes 393224 | tf_op jit(solution)/shard_map/ppermute | solution.py:21
  64.9 5.5 %collective-permute-start.12 = (bf16[64,1024]{1,0:T(8,128)(2,1)S(1)}, bf16[64,1024]{1,0:T(8,128)(2,1)S(1)}, u32[]{:S(2)}, u32[]{:S(2)}) collective-permute-start(bf16[64,1024]{1,0:T(8,128)(2,1)S(1)} %collective-permute-done.11), channel_id=1, source_target_pairs={{0,15},{1,0},{2,1},{3,2},{4,3},{5,4},{6,5},{7,6},{8,7},{9,8},{10,9... | collective-permute-start | bytes 393224 | tf_op jit(solution)/shard_map/ppermute | solution.py:23
  68.1 5.6 %collective-permute-start.6 = (bf16[64,1024]{1,0:T(8,128)(2,1)S(1)}, bf16[64,1024]{1,0:T(8,128)(2,1)S(1)}, u32[]{:S(2)}, u32[]{:S(2)}) collective-permute-start(bf16[64,1024]{1,0:T(8,128)(2,1)S(1)} %collective-permute-done.5), channel_id=1, source_target_pairs={{0,1},{1,2},{2,3},{3,4},{4,5},{5,6},{6,7},{7,8},{8,9},{9,10},{10,1... | collective-permute-start | bytes 393224 | tf_op jit(solution)/shard_map/ppermute | solution.py:21
  70.4 5.6 %collective-permute-start.13 = (bf16[64,1024]{1,0:T(8,128)(2,1)S(1)}, bf16[64,1024]{1,0:T(8,128)(2,1)S(1)}, u32[]{:S(2)}, u32[]{:S(2)}) collective-permute-start(bf16[64,1024]{1,0:T(8,128)(2,1)S(1)} %collective-permute-done.12), channel_id=1, source_target_pairs={{0,15},{1,0},{2,1},{3,2},{4,3},{5,4},{6,5},{7,6},{8,7},{9,8},{10,9... | collective-permute-start | bytes 393224 | tf_op jit(solution)/shard_map/ppermute | solution.py:23
  73.7 5.6 %collective-permute-start.7 = (bf16[64,1024]{1,0:T(8,128)(2,1)S(1)}, bf16[64,1024]{1,0:T(8,128)(2,1)S(1)}, u32[]{:S(2)}, u32[]{:S(2)}) collective-permute-start(bf16[64,1024]{1,0:T(8,128)(2,1)S(1)} %collective-permute-done.6), channel_id=1, source_target_pairs={{0,1},{1,2},{2,3},{3,4},{4,5},{5,6},{6,7},{7,8},{8,9},{9,10},{10,1... | collective-permute-start | bytes 393224 | tf_op jit(solution)/shard_map/ppermute | solution.py:21
  76.0 5.6 %collective-permute-start.14 = (bf16[64,1024]{1,0:T(8,128)(2,1)S(1)}, bf16[64,1024]{1,0:T(8,128)(2,1)S(1)}, u32[]{:S(2)}, u32[]{:S(2)}) collective-permute-start(bf16[64,1024]{1,0:T(8,128)(2,1)S(1)} %collective-permute-done.13), channel_id=1, source_target_pairs={{0,15},{1,0},{2,1},{3,2},{4,3},{5,4},{6,5},{7,6},{8,7},{9,8},{10,9... | collective-permute-start | bytes 393224 | tf_op jit(solution)/shard_map/ppermute | solution.py:23
  82.8 7.3 %collective-permute-start.15 = (bf16[256,128]{0,1:T(8,128)(2,1)S(1)}, bf16[256,128]{0,1:T(8,128)(2,1)S(1)}, u32[]{:S(2)}, u32[]{:S(2)}) collective-permute-start(bf16[256,128]{0,1:T(8,128)(2,1)S(1)} %get-tuple-element.226), channel_id=1, source_target_pairs={{0,16},{16,32},{32,48},{48,64},{64,80},{80,96},{96,112},{112,128},... | collective-permute-start | bytes 196616 | tf_op jit(solution)/shard_map/ppermute | solution.py:35
  86.1 6.2 %collective-permute-start.16 = (bf16[256,128]{0,1:T(8,128)(2,1)S(1)}, bf16[256,128]{0,1:T(8,128)(2,1)S(1)}, u32[]{:S(2)}, u32[]{:S(2)}) collective-permute-start(bf16[256,128]{0,1:T(8,128)(2,1)S(1)} %get-tuple-element.227), channel_id=1, source_target_pairs={{16,0},{32,16},{48,32},{64,48},{80,64},{96,80},{112,96},{128,112},... | collective-permute-start | bytes 196616 | tf_op jit(solution)/shard_map/ppermute | solution.py:36
  89.7 90.8 %all-gather.12.cloned.1.call-start = ((), (), s32[]{:S(2)}) async-start(), calls=%async_computation.3 | async-start | bytes 2228224 | tf_op jit(solution)/shard_map/all_gather | solution.py:153
  119.4 129.4 %reduce-scatter.2.cloned.1.call-start = ((), (), s32[]{:S(2)}) async-start(), calls=%async_computation.4 | async-start | bytes 2228224 | tf_op jit(solution)/shard_map/reduce_scatter | solution.py:159
  187.8 63.4 %copy-start.6 = (f32[1024]{0:T(1024)S(1)}, f32[1024]{0:T(1024)}, u32[]{:S(2)}) copy-start(f32[1024]{0:T(1024)} %param.27) | copy-start | bytes 12292
  187.8 63.4 %copy-start.7 = (f32[1024]{0:T(1024)S(1)}, f32[1024]{0:T(1024)}, u32[]{:S(2)}) copy-start(f32[1024]{0:T(1024)} %param.26) | copy-start | bytes 12292
  (13 other events, 222.1 us)
Sparse Core Ops, SparseCore 0:
  15.9 42.6 all-gather.9
  89.9 47.0 all-gather.13
  139.6 40.8 all-gather.11
  187.9 60.8 reduce-scatter.1
